TPU v7x, 512 devices: a whole 4x8x8 slice. The times are simulated.
512 devices in a mesh: src: 32 (over z_lo, x, core), tgt: 16 (over z_hi, y).
Axes of the slice: x: 4, y: 8, z: 8 (z_hi: 2, z_lo: 4; z = z_hi * 4 + z_lo), core: 2. Of those that a mesh axis runs over, the one named last changes fastest.
Arguments:
- src_embed: bfloat16 [8192, 1024], P('src', 'tgt'), as said below
- tgt_embed: bfloat16 [4096, 1024], P('tgt', 'src')
- src_near: int32 [8192, 16], P('src'), may hold values from 0 to 4095
- tgt_near: int32 [4096, 16], P('tgt'), may hold values from 0 to 8191
Outputs:
- margin: bfloat16 [8192, 4096], P('src', 'tgt')
- src_average: float32 [8192], P('src')
- tgt_average: float32 [4096], P('tgt')
Inputs may be any that keep to these rules, and one draw needn't show every extreme that they name: `src_embed`: every embedding is a sentence-specific multiple of one direction shared by both languages plus independent variation of comparable size, so that all cosines of the draw are positive.
All inputs are finite; a program needn't handle non-finite values.
Results may differ from a plain program's by a relative error of at most 0.001.
Values may be sent and summed in bfloat16 or wider, within the bound.
No kernel may reach another device: no remote copies, remote signals or barrier semaphores. Data moves between devices by JAX's collectives and lax.ppermute only.
A program may use at most 64 MiB of HBM per device.

v0:
```python
import jax
import jax.numpy as jnp
from jax import lax
from jax.sharding import PartitionSpec as P

EPSILON = 1e-06


def square_sums(values):
    wide = values.astype(jnp.float32)
    return jnp.sum(wide * wide, axis=1)


def local(src_embed, tgt_embed, src_near, tgt_near):
    src_index = lax.axis_index("src")
    tgt_index = lax.axis_index("tgt")
    source_rows = lax.all_gather(src_embed, "tgt", axis=1, tiled=True)
    src_count = source_rows.shape[0]
    tgt_count = tgt_embed.shape[0]
    near_count = src_near.shape[1]
    src_norm = jnp.sqrt(square_sums(source_rows) + EPSILON)
    contract = (((1,), (1,)), ((), ()))
    target_rows = lax.all_gather(tgt_embed, "src", axis=1, tiled=True)
    products = lax.dot_general(
        source_rows, target_rows, contract, preferred_element_type=jnp.float32
    )
    tgt_squares = square_sums(target_rows)
    tgt_norm = jnp.sqrt(tgt_squares + EPSILON)
    cosine_tile = products / (src_norm[:, None] * tgt_norm[None, :])
    local_targets = src_near - tgt_index * tgt_count
    local_sources = tgt_near - src_index * src_count
    target_iota = lax.broadcasted_iota(jnp.int32, (1, tgt_count), 1)
    source_iota = lax.broadcasted_iota(jnp.int32, (src_count, 1), 0)

    def add_neighbour(step, sums):
        row_sum, column_sum = sums
        wanted_target = lax.dynamic_slice_in_dim(local_targets, step, 1, 1)
        row_hits = wanted_target == target_iota
        row_sum = row_sum + jnp.sum(jnp.where(row_hits, cosine_tile, 0.0), axis=1)
        wanted_source = lax.dynamic_slice_in_dim(local_sources, step, 1, 1)
        column_hits = source_iota == wanted_source.reshape(1, tgt_count)
        column_sum = column_sum + jnp.sum(jnp.where(column_hits, cosine_tile, 0.0), axis=0)
        return (row_sum, column_sum)

    start_sums = (jnp.zeros((src_count,), jnp.float32), jnp.zeros((tgt_count,), jnp.float32))
    row_partial, column_partial = lax.fori_loop(0, near_count, add_neighbour, start_sums)
    src_average = lax.psum(row_partial, "tgt") / near_count
    tgt_average = lax.psum(column_partial, "src") / near_count
    margin = (cosine_tile / ((src_average[:, None] + tgt_average[None, :]) / 2.0)).astype(
        jnp.bfloat16
    )
    return (margin, src_average, tgt_average)


def solution(mesh):
    placed = (P("src", "tgt"), P("tgt", "src"), P("src", None), P("tgt", None))
    return jax.shard_map(
        local,
        mesh=mesh,
        in_specs=placed,
        out_specs=(P("src", "tgt"), P("src"), P("tgt")),
        check_vma=False,
    )
```

profile of v0, /device:TPU:8, one launch (start us, length us, event | category | flops | bytes accessed | tf_op | source)
XLA Modules:
  0.0 227.9 jit_solution(2381617098433261783)
XLA Ops:
  0.6 47.4 %all_gather.7 = bf16[256,1024]{0,1:T(8,128)(2,1)S(1)} all-gather(bf16[256,32]{0,1:T(8,128)(2,1)} %param.7), channel_id=1, replica_groups=mesh['src'=32,'tgt'=16] {'src'}, dimensions={1}, use_global_device_ids=true | all-gather | bytes 540672 | tf_op jit(solution)/shard_map/all_gather | solution.py:23
  48.2 0.6 copy-done
  48.8 51.3 %all_gather.6 = bf16[256,1024]{0,1:T(8,128)(2,1)S(1)} all-gather(bf16[256,64]{0,1:T(8,128)(2,1)S(1)} %copy-done), channel_id=1, replica_groups=mesh['src'=32,'tgt'=16] {'tgt'}, dimensions={1}, use_global_device_ids=true | all-gather | bytes 557056 | tf_op jit(solution)/shard_map/all_gather | solution.py:17
  100.2 0.3 multiply_divide_fusion
  100.6 0.4 copy-done.2
  101.0 0.3 copy-done.1
  101.3 4.0 %while.16 = (s32[]{:T(128)}, f32[256]{0:T(256)S(1)}, f32[256]{0:T(256)S(1)}, s32[256,16]{0,1:T(8,128)S(1)}, f32[256,256]{1,0:T(8,128)S(1)}, /*index=5*/s32[256,16]{0,1:T(8,128)S(1)}, s32[]{:T(128)}, s32[]{:T(128)}) while((s32[]{:T(128)}, f32[256]{0:T(256)S(1)}, f32[256]{0:T(256)S(1)}, s32[256,16]{0,1:T(8,128)S(1)}, ...), condition=%wide.region_5.6_spmd.clone, body=%wide.region_2.5_spmd.clone.sunk | while | flops 393731 | bytes 276583 | solution.py:46
  101.3 0.2 select_reduce_fusion.3
  101.6 0.2 select_reduce_fusion.3
  101.8 0.2 select_reduce_fusion.3
  102.1 0.2 select_reduce_fusion.3
  102.4 0.2 select_reduce_fusion.3
  102.6 0.2 select_reduce_fusion.3
  102.9 0.2 select_reduce_fusion.3
  103.1 0.2 select_reduce_fusion.3
  103.4 0.2 select_reduce_fusion.3
  103.6 0.2 select_reduce_fusion.3
  103.9 0.2 select_reduce_fusion.3
  104.1 0.2 select_reduce_fusion.3
  104.6 0.2 select_reduce_fusion.3
  104.9 0.2 select_reduce_fusion.3
  105.3 67.4 %psum.15 = f32[256]{0:T(256)S(1)} all-reduce(f32[256]{0:T(256)S(1)} %get-tuple-element.144), channel_id=1, replica_groups=mesh['src'=32,'tgt'=16] {'src'}, use_global_device_ids=true, to_apply=%region_7.8 | all-reduce | flops 256 | bytes 2048 | tf_op jit(solution)/shard_map/psum | solution.py:48
  172.7 54.4 %psum.14 = f32[256]{0:T(256)S(1)} all-reduce(f32[256]{0:T(256)S(1)} %get-tuple-element.143), channel_id=1, replica_groups=mesh['src'=32,'tgt'=16] {'tgt'}, use_global_device_ids=true, to_apply=%region_6.7 | all-reduce | flops 256 | bytes 2048 | tf_op jit(solution)/shard_map/psum | solution.py:47
  227.1 0.8 fusion.5
  (66 shorter events, 1.3 us)
Async XLA Ops:
  48.0 0.8 copy-start
  100.2 0.7 copy-start.2
  100.6 0.7 copy-start.1
  172.7 54.4 %copy-start.3 = (f32[256]{0:T(256)}, f32[256]{0:T(256)S(1)}, u32[]{:S(2)}) copy-start(f32[256]{0:T(256)S(1)} %broadcast_multiply_fusion) | copy-start | bytes 3076
  227.1 0.8 copy-start.4
where the time goes:
time: 228 us
  blocking collectives  220 us (96%)
  other arithmetic  4.33 us (2%)
    psum x1, blocking collectives, local(): tgt_average = lax.psum(column_partial, 'src') / near_count  67.4 us
    psum x1, blocking collectives, local(): src_average = lax.psum(row_partial, 'tgt') / near_count  54.4 us
    all_gather x1, blocking collectives, local(): source_rows = lax.all_gather(src_embed, 'tgt', axis=1, tiled=True)  51.3 us
    all_gather x1, blocking collectives, local(): target_rows = lax.all_gather(tgt_embed, 'src', axis=1, tiled=True)  47.4 us

commit v1 on v0

--- a/solution.py
+++ b/solution.py
@@ -1,9 +1,17 @@
+import functools
 import jax
 import jax.numpy as jnp
 from jax import lax
 from jax.sharding import PartitionSpec as P
 
 EPSILON = 1e-06
+
+
+def test_the_waves(vector, group_axis):
+    return jnp.sum(lax.all_gather(vector, group_axis), axis=0)
+
+
+cut_the_flows = functools.partial(test_the_waves, group_axis="src")
 
 
 def square_sums(values):
@@ -45,7 +53,7 @@
     start_sums = (jnp.zeros((src_count,), jnp.float32), jnp.zeros((tgt_count,), jnp.float32))
     row_partial, column_partial = lax.fori_loop(0, near_count, add_neighbour, start_sums)
     src_average = lax.psum(row_partial, "tgt") / near_count
-    tgt_average = lax.psum(column_partial, "src") / near_count
+    tgt_average = cut_the_flows(column_partial) / near_count
     margin = (cosine_tile / ((src_average[:, None] + tgt_average[None, :]) / 2.0)).astype(
         jnp.bfloat16
     )

time: 228 us -> 199 us (0.87)
  the two profiles are of different devices: /device:TPU:8 before, /device:TPU:10 now
where the time goes in v1:
time: 199 us
  blocking collectives  191 us (96%)
  other arithmetic  4.39 us (2%)
    psum x1, blocking collectives, local(): src_average = lax.psum(row_partial, 'tgt') / near_count  54.4 us
    all_gather x1, blocking collectives, local(): source_rows = lax.all_gather(src_embed, 'tgt', axis=1, tiled=True)  51 us
    all_gather x1, blocking collectives, test_the_waves(): return jnp.sum(lax.all_gather(vector, group_axis), axis=0)  42.9 us
    all_gather x1, blocking collectives, local(): target_rows = lax.all_gather(tgt_embed, 'src', axis=1, tiled=True)  42.8 us

profile of v1, /device:TPU:10, one launch (start us, length us, event | category | flops | bytes accessed | tf_op | source)
XLA Modules:
  0.0 198.7 jit_solution(6658642173173271684)
XLA Ops:
  0.6 42.8 %all_gather.13 = bf16[256,1024]{0,1:T(8,128)(2,1)S(1)} all-gather(bf16[256,32]{0,1:T(8,128)(2,1)} %param.7), channel_id=1, replica_groups=mesh['src'=32,'tgt'=16] {'src'}, dimensions={1}, use_global_device_ids=true | all-gather | bytes 540672 | tf_op jit(solution)/shard_map/all_gather | solution.py:31
  43.6 0.6 copy-done
  44.2 51.0 %all_gather.12 = bf16[256,1024]{0,1:T(8,128)(2,1)S(1)} all-gather(bf16[256,64]{0,1:T(8,128)(2,1)S(1)} %copy-done), channel_id=1, replica_groups=mesh['src'=32,'tgt'=16] {'tgt'}, dimensions={1}, use_global_device_ids=true | all-gather | bytes 557056 | tf_op jit(solution)/shard_map/all_gather | solution.py:25
  95.4 0.3 multiply_divide_fusion
  95.8 0.4 copy-done.2
  96.1 0.4 copy-done.1
  96.5 4.0 %while.16 = (s32[]{:T(128)}, f32[256]{0:T(256)S(1)}, f32[256]{0:T(256)S(1)}, s32[256,16]{0,1:T(8,128)S(1)}, f32[256,256]{1,0:T(8,128)S(1)}, /*index=5*/s32[256,16]{0,1:T(8,128)S(1)}, s32[]{:T(128)}, s32[]{:T(128)}) while((s32[]{:T(128)}, f32[256]{0:T(256)S(1)}, f32[256]{0:T(256)S(1)}, s32[256,16]{0,1:T(8,128)S(1)}, ...), condition=%wide.region_5.6_spmd.clone, body=%wide.region_2.5_spmd.clone.sunk | while | flops 393731 | bytes 276583 | solution.py:54
  96.5 0.2 select_reduce_fusion.3
  96.8 0.2 select_reduce_fusion.3
  97.0 0.2 select_reduce_fusion.3
  97.3 0.2 select_reduce_fusion.3
  97.5 0.2 select_reduce_fusion.3
  97.8 0.2 select_reduce_fusion.3
  98.0 0.2 select_reduce_fusion.3
  98.3 0.2 select_reduce_fusion.3
  98.5 0.2 select_reduce_fusion.3
  98.8 0.2 select_reduce_fusion.3
  99.0 0.2 select_reduce_fusion.3
  99.3 0.2 select_reduce_fusion.3
  100.0 0.2 select_reduce_fusion.3
  100.3 0.2 select_reduce_fusion.3
  100.5 42.9 %all-gather.1 = f32[32,1,256]{2,1,0:T(1,128)S(1)} all-gather(f32[1,1,256]{2,1,0:T(1,128)S(1)} %bitcast.11), channel_id=2, replica_groups=mesh['src'=32,'tgt'=16] {'src'}, dimensions={0}, use_global_device_ids=true | all-gather | bytes 33792 | tf_op jit(solution)/shard_map/all_gather | solution.py:11
  143.5 54.4 %psum.7 = f32[256]{0:T(256)S(1)} all-reduce(f32[256]{0:T(256)S(1)} %get-tuple-element.143), channel_id=1, replica_groups=mesh['src'=32,'tgt'=16] {'tgt'}, use_global_device_ids=true, to_apply=%region_6.7 | all-reduce | flops 256 | bytes 2048 | tf_op jit(solution)/shard_map/psum | solution.py:55
  197.9 0.8 fusion.5
  (67 shorter events, 1.4 us)
Async XLA Ops:
  43.4 0.8 copy-start
  95.4 0.7 copy-start.2
  95.8 0.7 copy-start.1
  143.5 54.4 %copy-start.3 = (f32[256]{0:T(256)}, f32[256]{0:T(256)S(1)}, u32[]{:S(2)}) copy-start(f32[256]{0:T(256)S(1)} %broadcast_multiply_fusion) | copy-start | bytes 3076
  197.9 0.8 copy-start.4

commit v2 on v0

--- a/solution.py
+++ b/solution.py
@@ -4,6 +4,13 @@
 from jax.sharding import PartitionSpec as P
 
 EPSILON = 1e-06
+
+
+def all_by_exchange(x, axis, dim):
+    size = lax.axis_size(axis)
+    blocks = jnp.stack([x for _ in range(size)])
+    blocks = lax.all_to_all(blocks, axis, split_axis=0, concat_axis=0)
+    return jnp.concatenate(blocks, axis=dim)
 
 
 def square_sums(values):
@@ -14,7 +21,7 @@
 def local(src_embed, tgt_embed, src_near, tgt_near):
     src_index = lax.axis_index("src")
     tgt_index = lax.axis_index("tgt")
-    source_rows = lax.all_gather(src_embed, "tgt", axis=1, tiled=True)
+    source_rows = all_by_exchange(src_embed, "tgt", 1)
     src_count = source_rows.shape[0]
     tgt_count = tgt_embed.shape[0]
     near_count = src_near.shape[1]

time: 228 us -> 190 us (0.83)
  the two profiles are of different devices: /device:TPU:8 before, /device:TPU:0 now
where the time goes in v2:
time: 190 us
  blocking collectives  171 us (90%)
  starting transfers between devices  10.3 us (5%)
  other arithmetic  4.33 us (2%)
  local copies, waits for them, and re-layouts  3.19 us (2%)
    psum x1, blocking collectives, local(): tgt_average = lax.psum(column_partial, 'src') / near_count  67.7 us
    psum x1, blocking collectives, local(): src_average = lax.psum(row_partial, 'tgt') / near_count  56.1 us
    all_gather x1, blocking collectives, local(): target_rows = lax.all_gather(tgt_embed, 'src', axis=1, tiled=True)  46.7 us
    all_to_all x1, starting transfers between devices, all_by_exchange(): blocks = lax.all_to_all(blocks, axis, split_axis=0, concat_axis=0)  10.3 us
  transfers between devices with their start and end apart: 1, of which 0 were waited for; matrix products, arithmetic and copies ran while one was open for 0% of the time, Pallas kernels for 0%

profile of v2, /device:TPU:0, one launch (start us, length us, event | category | flops | bytes accessed | tf_op | source)
XLA Modules:
  0.0 189.9 jit_solution(9432345069644469771)
XLA Ops:
  0.6 1.6 stack.2
  2.2 10.3 %all-to-all-start = ((bf16[16,256,64]{1,2,0:T(8,128)(2,1)}), bf16[16,256,64]{1,2,0:T(8,128)(2,1)S(1)}, u32[]{:S(2)}, u32[]{:S(2)}) async-start(bf16[16,256,64]{1,2,0:T(8,128)(2,1)} %stack.2), calls=%async_computation | async-start | bytes 1048576 | tf_op jit(solution)/shard_map/all_to_all | solution.py:12
  12.6 0.7 copy-done
  13.2 46.7 %all_gather.3 = bf16[256,1024]{0,1:T(8,128)(2,1)S(1)} all-gather(bf16[256,32]{0,1:T(8,128)(2,1)S(1)} %copy-done), channel_id=1, replica_groups=mesh['src'=32,'tgt'=16] {'src'}, dimensions={1}, use_global_device_ids=true | all-gather | bytes 540672 | tf_op jit(solution)/shard_map/all_gather | solution.py:30
  60.1 0.5 copy-done.1
  60.8 0.3 multiply_divide_fusion
  61.2 4.0 %while.16 = (s32[]{:T(128)}, f32[256]{0:T(256)S(1)}, f32[256]{0:T(256)S(1)}, s32[256,16]{0,1:T(8,128)S(1)}, f32[256,256]{1,0:T(8,128)S(1)}, /*index=5*/s32[256,16]{0,1:T(8,128)S(1)}, s32[]{:T(128)}, s32[]{:T(128)}) while((s32[]{:T(128)}, f32[256]{0:T(256)S(1)}, f32[256]{0:T(256)S(1)}, s32[256,16]{0,1:T(8,128)S(1)}, ...), condition=%wide.region_5.6_spmd.clone, body=%wide.region_2.5_spmd.clone.sunk | while | flops 393731 | bytes 276583 | solution.py:53
  61.2 0.2 select_reduce_fusion.3
  61.5 0.2 select_reduce_fusion.3
  61.7 0.2 select_reduce_fusion.3
  62.0 0.2 select_reduce_fusion.3
  62.2 0.2 select_reduce_fusion.3
  62.5 0.2 select_reduce_fusion.3
  62.8 0.2 select_reduce_fusion.3
  63.0 0.2 select_reduce_fusion.3
  63.3 0.2 select_reduce_fusion.3
  63.5 0.2 select_reduce_fusion.3
  63.8 0.2 select_reduce_fusion.3
  64.0 0.2 select_reduce_fusion.3
  64.3 0.2 select_reduce_fusion.3
  64.5 0.2 select_reduce_fusion.3
  65.2 67.7 %psum.15 = f32[256]{0:T(256)S(1)} all-reduce(f32[256]{0:T(256)S(1)} %get-tuple-element.144), channel_id=1, replica_groups=mesh['src'=32,'tgt'=16] {'src'}, use_global_device_ids=true, to_apply=%region_7.8 | all-reduce | flops 256 | bytes 2048 | tf_op jit(solution)/shard_map/psum | solution.py:55
  133.0 56.1 %psum.14 = f32[256]{0:T(256)S(1)} all-reduce(f32[256]{0:T(256)S(1)} %get-tuple-element.143), channel_id=1, replica_groups=mesh['src'=32,'tgt'=16] {'tgt'}, use_global_device_ids=true, to_apply=%region_6.7 | all-reduce | flops 256 | bytes 2048 | tf_op jit(solution)/shard_map/psum | solution.py:54
  189.1 0.8 fusion.5
  (68 shorter events, 1.3 us)
Async XLA Ops:
  2.2 58.4 %all-to-all-start = ((bf16[16,256,64]{1,2,0:T(8,128)(2,1)}), bf16[16,256,64]{1,2,0:T(8,128)(2,1)S(1)}, u32[]{:S(2)}, u32[]{:S(2)}) async-start(bf16[16,256,64]{1,2,0:T(8,128)(2,1)} %stack.2), calls=%async_computation | async-start | bytes 1048576 | tf_op jit(solution)/shard_map/all_to_all | solution.py:12
  12.5 0.7 copy-start
  59.9 0.7 copy-start.1
  59.9 0.7 copy-start.2
  133.0 56.1 %copy-start.3 = (f32[256]{0:T(256)}, f32[256]{0:T(256)S(1)}, u32[]{:S(2)}) copy-start(f32[256]{0:T(256)S(1)} %broadcast_multiply_fusion) | copy-start | bytes 3076
  189.1 0.8 copy-start.4
